TPU v7x, 32 devices: a whole 2x2x4 slice. The times are simulated.
32 devices in a mesh: groups: 2 (over y), row: 4 (over z), col: 2 (over x), chan: 2 (over core).
Axes of the slice: x: 2, y: 2, z: 4, core: 2. Of those that a mesh axis runs over, the one named last changes fastest.
Arguments:
- pair: bfloat16 [128, 64, 128], P(('groups', 'row'), 'col', 'chan'), parts along dimension 0, may hold values from -6 to 6
- token_mask: int32 [128], P('groups'), parts along dimension 0, may hold values 0 or 1
- w_proj: bfloat16 [2, 4, 128, 128], P(None, None, None, 'chan'), may hold values from -0.5 to 0.5
- w_gate: bfloat16 [2, 128, 128], replicated, may hold values from -0.5 to 0.5
- w_out: bfloat16 [2, 128, 128], replicated, may hold values from -0.5 to 0.5
- in_gain: float32 [2, 128], replicated, may hold values from 0.5 to 1.5
- in_bias: float32 [2, 128], replicated, may hold values from -3 to 3
- out_gain: float32 [2, 128], replicated, may hold values from 0.5 to 1.5
- out_bias: float32 [2, 128], replicated, may hold values from -3 to 3
Outputs:
- updated: bfloat16 [128, 64, 128], P(('groups', 'row'), 'col', 'chan'), parts along dimension 0
There are 2 independent parts, one for each index of `groups`. A program takes and returns all parts, laid end to end along the dimension named above; an argument that names none is the same for every part. Nothing has to cross between parts.
Inputs may be any that keep to these rules, and one draw needn't show every extreme that they name: `token_mask`: 1 marks a real token, 0 a padded one.
All inputs are finite; a program needn't handle non-finite values.
Results may differ from a plain program's by a relative error of at most 0.009.
Values may be sent and summed in bfloat16 or wider, within the bound.
A program may use at most 64 MiB of HBM per device.

v0:
```python
import jax
import jax.numpy as jnp
from jax import lax
from jax.sharding import PartitionSpec as P

epsilon = 1e-05


def broadcast(value, axis, source):
    kept = jnp.where(lax.axis_index(axis) == source, value, 0).astype(value.dtype)
    return lax.psum(kept, axis)


def normalize(values, gain, bias):
    center = jnp.mean(values, axis=-1, keepdims=True)
    spread = jnp.mean(jnp.square(values - center), axis=-1, keepdims=True)
    return (values - center) * lax.rsqrt(spread + epsilon) * gain + bias


def widen(values):
    return lax.all_gather(values, "chan", axis=2, tiled=True)


def local(pair, token_mask, w_proj, w_gate, w_out, in_gain, in_bias, out_gain, out_bias):
    row_devices = lax.axis_size("row")
    col_devices = lax.axis_size("col")
    chan_devices = lax.axis_size("chan")
    row_count, col_count, chan_share = pair.shape
    ratio = row_devices // col_devices
    hidden_share = w_proj.shape[3]
    hidden_all = hidden_share * chan_devices
    row_index = lax.axis_index("row")
    col_index = lax.axis_index("col")
    chan_index = lax.axis_index("chan")
    masked = token_mask.astype(jnp.float32)
    row_mask = lax.dynamic_slice_in_dim(masked, row_index * row_count, row_count)
    col_mask = lax.dynamic_slice_in_dim(masked, col_index * col_count, col_count)
    pair_mask = (row_mask[:, None] * col_mask[None, :])[:, :, None]
    own_pair = pair
    full_pair = widen(pair)
    for direction in range(2):
        normed = normalize(
            full_pair.astype(jnp.float32), in_gain[direction], in_bias[direction]
        ).astype(jnp.bfloat16)
        projected_in = jnp.einsum(
            "ijc,wch->wijh", normed, w_proj[direction], preferred_element_type=jnp.float32
        )
        left = (jax.nn.sigmoid(projected_in[1]) * projected_in[0] * pair_mask).astype(jnp.bfloat16)
        right = (jax.nn.sigmoid(projected_in[3]) * projected_in[2] * pair_mask).astype(jnp.bfloat16)
        if direction == 0:
            right_wide = lax.all_gather(right, "col", axis=1, tiled=True)
            pieces = []
            for piece_index in range(ratio):
                pieces.append(broadcast(right_wide, "row", col_index * ratio + piece_index))
            right_panel = jnp.concatenate(pieces, axis=0)
            mixed = jnp.einsum(
                "ikh,jkh->ijh",
                lax.all_gather(left, "col", axis=1, tiled=True),
                right_panel,
                preferred_element_type=jnp.float32,
            )
        else:
            left_cols = lax.all_gather(left, "row", axis=0, tiled=True)
            column_block = lax.dynamic_slice_in_dim(
                left_cols, row_index % ratio * row_count, row_count, 1
            )
            left_panel = broadcast(column_block, "col", row_index // ratio)
            mixed = jnp.einsum(
                "kih,kjh->ijh",
                left_panel,
                lax.all_gather(right, "row", axis=0, tiled=True),
                preferred_element_type=jnp.float32,
            )
        mixed = mixed.astype(jnp.bfloat16)
        mixed_wide = mixed.astype(jnp.float32)
        totals, squares = lax.psum(
            (jnp.sum(mixed_wide, axis=-1), jnp.sum(mixed_wide * mixed_wide, axis=-1)), "chan"
        )
        center = (totals / hidden_all)[:, :, None]
        spread = (squares / hidden_all)[:, :, None] - center * center
        gain_own = lax.dynamic_slice_in_dim(
            out_gain[direction], chan_index * hidden_share, hidden_share
        )
        bias_own = lax.dynamic_slice_in_dim(
            out_bias[direction], chan_index * hidden_share, hidden_share
        )
        mixed_norm = (
            (mixed_wide - center) * lax.rsqrt(spread + epsilon) * gain_own + bias_own
        ).astype(jnp.bfloat16)
        out_rows = lax.dynamic_slice_in_dim(
            w_out[direction], chan_index * hidden_share, hidden_share, 0
        )
        partial_out = jnp.einsum(
            "ijh,hc->ijc", mixed_norm, out_rows, preferred_element_type=jnp.float32
        )
        projected = lax.psum_scatter(partial_out, "chan", scatter_dimension=2, tiled=True)
        gate_cols = lax.dynamic_slice_in_dim(
            w_gate[direction], chan_index * chan_share, chan_share, 1
        )
        gate = jax.nn.sigmoid(
            jnp.einsum("ijc,ce->ije", normed, gate_cols, preferred_element_type=jnp.float32)
        )
        own_pair = (own_pair.astype(jnp.float32) + gate * projected).astype(jnp.bfloat16)
        if direction == 0:
            full_pair = widen(own_pair)
    return own_pair


def solution(mesh):
    return jax.shard_map(
        local,
        mesh=mesh,
        in_specs=(
            P(("groups", "row"), "col", "chan"),
            P("groups"),
            P(None, None, None, "chan"),
            P(),
            P(),
            P(),
            P(),
            P(),
            P(),
        ),
        out_specs=P(("groups", "row"), "col", "chan"),
        check_vma=False,
    )
```

profile of v0, /device:TPU:0, one launch (start us, length us, event | category | flops | bytes accessed | tf_op | source)
XLA Modules:
  0.0 148.4 jit_solution(15098952179707264425)
XLA Ops:
  6.5 0.7 copy-done.8
  7.2 0.1 dynamic_slice.44
  7.3 0.1 dynamic_slice.43
  7.3 1.1 copy.42
  8.5 2.3 %all_gather.18 = bf16[16,32,128]{1,0,2:T(8,128)(2,1)S(1)} all-gather(bf16[16,32,64]{1,0,2:T(8,128)(2,1)S(1)} %copy.42), channel_id=1, replica_groups=mesh['groups'=2,'row'=4,'col'=2,'chan'=2] {'chan'}, dimensions={2}, use_global_device_ids=true | all-gather | bytes 196608 | tf_op jit(solution)/shard_map/all_gather | solution.py:21
  10.8 0.4 copy.43
  11.2 0.1 convert_reduce_fusion.1
  11.4 0.3 fusion.24
  11.7 0.6 copy-done.6
  12.3 0.1 broadcast_multiply_fusion
  12.4 0.4 convolution_bitcast_fusion.1
  12.8 0.2 fusion.42
  12.9 7.3 %all_gather.19 = bf16[16,64,64]{2,1,0:T(8,128)(2,1)S(1)} all-gather(bf16[16,32,64]{2,1,0:T(8,128)(2,1)S(1)} %get-tuple-element.18), channel_id=1, replica_groups=mesh['groups'=2,'row'=4,'col'=2,'chan'=2] {'col'}, dimensions={1}, use_global_device_ids=true | all-gather | bytes 196608 | tf_op jit(solution)/shard_map/all_gather | solution.py:51
  20.3 0.8 broadcast_select_fusion.2
  21.1 0.0 all-reduce.8.cloned.1.call-update
  21.1 0.0 reduce-scatter.7.cloned.1.call-start
  21.2 0.7 copy-done.4
  21.9 0.7 copy-done.5
  22.6 0.1 fusion.82
  22.6 5.7 %all_gather.20 = bf16[16,64,64]{2,1,0:T(8,128)(2,1)S(1)} all-gather(bf16[16,32,64]{2,1,0:T(8,128)(2,1)S(1)} %get-tuple-element.17), channel_id=1, replica_groups=mesh['groups'=2,'row'=4,'col'=2,'chan'=2] {'col'}, dimensions={1}, use_global_device_ids=true | all-gather | bytes 196608 | tf_op jit(solution)/shard_map/all_gather | solution.py:58
  28.3 0.3 copy.50
  28.6 0.6 copy-done.2
  29.2 32.1 %all-reduce.8.cloned.1.call-done = (bf16[16,64,64]{2,1,0:T(8,128)(2,1)}, bf16[16,64,64]{2,1,0:T(8,128)(2,1)}) async-done(((bf16[16,64,64]{2,1,0:T(8,128)(2,1)}, bf16[16,64,64]{2,1,0:T(8,128)(2,1)}), (bf16[16,64,64]{2,1,0:T(8,128)(2,1)}, bf16[16,64,64]{2,1,0:T(8,128)(2,1)})) %all-reduce.8.cloned.1.call-update) | async-done | bytes 262160 | tf_op jit(solution)/shard_map/psum | solution.py:11
  61.3 1.1 pad_maximum_fusion
  62.4 0.8 copy.49
  63.2 0.4 fusion.87
  63.6 3.3 %all-reduce.1 = (f32[16,32]{1,0:T(8,128)S(1)}, f32[16,32]{1,0:T(8,128)S(1)}) all-reduce(f32[16,32]{1,0:T(8,128)S(1)} %get-tuple-element.8, f32[16,32]{1,0:T(8,128)S(1)} %get-tuple-element.7), channel_id=1, replica_groups=mesh['groups'=2,'row'=4,'col'=2,'chan'=2] {'chan'}, use_global_device_ids=true, to_apply=%region_7.8 | all-reduce | flops 1024 | bytes 8192 | tf_op jit(solution)/shard_map/psum | solution.py:76
  66.9 0.2 add_convert_fusion.1
  67.1 0.2 fusion.58
  67.4 0.5 copy.62
  67.9 1.1 reshape.119
  68.9 0.0 reduce-scatter.7.cloned.1.call-update
  69.0 0.0 all-reduce.6.cloned.1.call-start
  69.1 0.7 copy-done.3
  69.8 6.9 %reduce-scatter.7.cloned.1.call-done = f32[64,512]{1,0:T(8,128)} async-done(((f32[128,512]{1,0:T(8,128)}), f32[64,512]{1,0:T(8,128)}) %reduce-scatter.7.cloned.1.call-update) | async-done | bytes 131088
  76.7 1.1 reshape.120
  77.8 0.2 copy.63
  78.1 0.6 copy-done
  78.7 0.3 fusion.14
  79.1 0.3 copy.52
  79.3 2.2 %all_gather.21 = bf16[16,32,128]{1,0,2:T(8,128)(2,1)S(1)} all-gather(bf16[16,32,64]{1,0,2:T(8,128)(2,1)S(1)} %copy.52), channel_id=1, replica_groups=mesh['groups'=2,'row'=4,'col'=2,'chan'=2] {'chan'}, dimensions={2}, use_global_device_ids=true | all-gather | bytes 196608 | tf_op jit(solution)/shard_map/all_gather | solution.py:21
  81.5 0.4 copy.53
  81.9 0.1 convert_reduce_fusion
  82.1 0.3 fusion.20
  82.4 0.4 convolution_bitcast_fusion
  82.7 0.2 fusion.30
  82.9 16.3 %all_gather.23 = bf16[64,32,64]{2,1,0:T(8,128)(2,1)S(1)} all-gather(bf16[16,32,64]{2,1,0:T(8,128)(2,1)S(1)} %get-tuple-element.16), channel_id=1, replica_groups=mesh['groups'=2,'row'=4,'col'=2,'chan'=2] {'row'}, dimensions={0}, use_global_device_ids=true | all-gather | bytes 327680 | tf_op jit(solution)/shard_map/all_gather | solution.py:63
  99.2 0.4 copy.69
  99.6 0.7 broadcast_select_fusion
  100.4 0.0 reduce-scatter.9.cloned.1.call-start
  100.4 0.1 fusion.84
  100.5 16.0 %all_gather.22 = bf16[64,32,64]{2,1,0:T(8,128)(2,1)S(1)} all-gather(bf16[16,32,64]{2,1,0:T(8,128)(2,1)S(1)} %get-tuple-element.15), channel_id=1, replica_groups=mesh['groups'=2,'row'=4,'col'=2,'chan'=2] {'row'}, dimensions={0}, use_global_device_ids=true | all-gather | bytes 327680 | tf_op jit(solution)/shard_map/all_gather | solution.py:71
  116.5 1.6 %copy.57 = bf16[64,32,64]{1,0,2:T(8,128)(2,1)S(1)} copy(bf16[64,32,64]{2,1,0:T(8,128)(2,1)S(1)} %all_gather.22) | data formatting | bytes 524288 | tf_op jit(solution)/shard_map/all_gather | solution.py:71
  118.1 6.9 %all-reduce.6.cloned.1.call-done = bf16[64,16,64]{0,1,2:T(8,128)(2,1)} async-done(((bf16[64,16,64]{0,1,2:T(8,128)(2,1)}), bf16[64,16,64]{0,1,2:T(8,128)(2,1)}) %all-reduce.6.cloned.1.call-update) | async-done | bytes 131088 | tf_op jit(solution)/shard_map/psum | solution.py:11
  125.0 1.3 fusion.86
  126.4 3.3 %all-reduce = (f32[16,32]{1,0:T(8,128)S(1)}, f32[16,32]{1,0:T(8,128)S(1)}) all-reduce(f32[16,32]{1,0:T(8,128)S(1)} %get-tuple-element.6, f32[16,32]{1,0:T(8,128)S(1)} %get-tuple-element.5), channel_id=1, replica_groups=mesh['groups'=2,'row'=4,'col'=2,'chan'=2] {'chan'}, use_global_device_ids=true, to_apply=%region_15.16 | all-reduce | flops 1024 | bytes 8192 | tf_op jit(solution)/shard_map/psum | solution.py:76
  129.7 0.2 add_convert_fusion
  129.9 0.2 fusion.56
  130.1 0.5 copy.64
  130.6 1.1 reshape.121
  131.7 7.8 %reduce-scatter.9.cloned.1.call-done = f32[64,512]{1,0:T(8,128)} async-done(((f32[128,512]{1,0:T(8,128)}), f32[64,512]{1,0:T(8,128)}) %reduce-scatter.9.cloned.1.call-update) | async-done | bytes 131088
  139.6 1.1 reshape.122
  140.6 0.2 copy.65
  140.9 1.0 fusion.15
  (27 shorter events, 0.2 us)
Async XLA Ops:
  6.5 54.8 %all-reduce.8.cloned.1.call-start = ((), (), s32[]{:S(2)}) async-start(), calls=%async_computation.5 | async-start | bytes 1048576 | tf_op jit(solution)/shard_map/psum | solution.py:11
  6.5 0.7 copy-start.8
  11.3 1.1 copy-start.1
  11.6 0.7 copy-start.6
  11.6 0.7 copy-start.7
  21.1 55.6 %reduce-scatter.7.cloned.1.call-start = ((), (), s32[]{:S(2)}) async-start(), calls=%async_computation.3 | async-start | bytes 393216
  21.2 0.7 copy-start.4
  21.9 0.7 copy-start.5
  28.3 0.8 copy-start.2
  68.9 0.8 copy-start.3
  69.0 56.0 %all-reduce.6.cloned.1.call-start = ((), (), s32[]{:S(2)}) async-start(), calls=%async_computation.2 | async-start | bytes 524288 | tf_op jit(solution)/shard_map/psum | solution.py:11
  77.8 0.9 copy-start
  100.4 39.2 %reduce-scatter.9.cloned.1.call-start = ((), (), s32[]{:S(2)}) async-start(), calls=%async_computation.4 | async-start | bytes 393216
Sparse Core Ops, SparseCore 0:
  21.3 40.0 all-reduce.7
  69.1 7.5 reduce-scatter.6
  100.5 24.4 all-reduce.5
  131.8 7.6 reduce-scatter.8
where the time goes:
time: 149 us; the launch traced here: 148 us
  blocking collectives  56.3 us (38%)
  waiting for transfers between devices  53.9 us (36%)
  local copies, waits for them, and re-layouts  16 us (11%)
  between operations  13.4 us (9%)
  other arithmetic  4.38 us (3%)
  matrix products  4.27 us (3%)
    psum x2, waiting for transfers between devices, broadcast(): return lax.psum(kept, axis)  39 us
    all_gather x1, blocking collectives, local(): left_cols = lax.all_gather(left, 'row', axis=0, tiled=True)  16.3 us
    all_gather x1, blocking collectives, local(): lax.all_gather(right, 'row', axis=0, tiled=True)  16 us
    unnamed x6, waiting for transfers between devices  14.8 us
    unnamed x28, local copies, waits for them, and re-layouts  12 us
    all_gather x1, blocking collectives, local(): right_wide = lax.all_gather(right, 'col', axis=1, tiled=True)  7.31 us
    psum x2, blocking collectives, local(): lax.psum((jnp.sum(mixed_wide, axis=-1), jnp.sum(mixed_wide * mixed_wide,...  6.59 us
    all_gather x1, blocking collectives, local(): lax.all_gather(left, 'col', axis=1, tiled=True)  5.69 us
  transfers between devices with their start and end apart: 4, of which 4 were waited for; matrix products, arithmetic and copies ran while one was open for 1% of the time, Pallas kernels for 0%

commit v1 on v0

v1 whole, which is shorter than its diff:
```python
import functools

import jax
import jax.numpy as jnp
from jax import lax
from jax.experimental import pallas as pl
from jax.experimental.pallas import tpu as pltpu
from jax.sharding import PartitionSpec as P

epsilon = 1e-05
MESH = pl.DeviceIdType.MESH


def normalize(values, gain, bias):
    center = jnp.mean(values, axis=-1, keepdims=True)
    off = values - center
    spread = jnp.mean(off * off, axis=-1, keepdims=True)
    return off * lax.rsqrt(spread + epsilon) * gain + bias


def sigmoid(values):
    return 0.5 * jnp.tanh(0.5 * values) + 0.5


def kernel(
    rows, cols, chans, edge,
    pair_ref, mask_ref, w_proj_ref, w_gate_ref, w_out_ref,
    in_gain_ref, in_bias_ref, out_gain_ref, out_bias_ref, out_ref,
    raw, mid, fin, w_half, w_full, mask_col, spread_op, tile_op, values, normed_own,
    send_sems, raw_sems, mid_sems, w_sems, fin_sems,
):
    group = lax.axis_index("groups")
    r, c, h = lax.axis_index("row"), lax.axis_index("col"), lax.axis_index("chan")
    blocks = rows
    area = edge * edge
    length = edge * blocks
    half = pair_ref.shape[2]
    q = c * chans + h
    away = jnp.where(q == r, 0, 1)
    off_diagonal = q != r
    sibling = (group, r, c, 1 - h)

    def plane(step):
        other = lax.rem(q + step, blocks)
        return (group, r, other // chans, lax.rem(other, chans))

    def column(step):
        return (group, lax.rem(r + step, rows), r // chans, lax.rem(r, chans))

    barrier = pltpu.get_barrier_semaphore()
    for step in range(1, blocks):
        pl.semaphore_signal(barrier, inc=1, device_id=plane(step), device_id_type=MESH)

    @pl.when(off_diagonal)
    def _():
        for other in range(blocks):
            pl.semaphore_signal(
                barrier, inc=1,
                device_id=(group, q, other // chans, other % chans), device_id_type=MESH,
            )

    own = pair_ref[...].astype(jnp.float32)
    packed = jnp.concatenate([own[:, :edge, :], own[:, edge:, :]], axis=-1)
    raw[0, q] = packed.reshape(area, 2 * half).astype(jnp.bfloat16)
    pl.semaphore_wait(barrier, 2 * (blocks - 1))

    def send_block(buffer, sems, base):
        copies = []
        for step in range(1, blocks):
            copies.append(pltpu.make_async_remote_copy(
                src_ref=buffer.at[0, q], dst_ref=buffer.at[1, q],
                send_sem=send_sems.at[base + step], recv_sem=sems.at[1, q],
                device_id=column(step), device_id_type=MESH,
            ))
        for step in range(1, blocks):
            copies.append(pltpu.make_async_remote_copy(
                src_ref=buffer.at[0, q], dst_ref=buffer.at[0, q],
                send_sem=send_sems.at[base + blocks + step], recv_sem=sems.at[0, q],
                device_id=plane(step), device_id_type=MESH,
            ))
        for copy in copies:
            copy.start()
        return copies

    def wait_block(buffer, sems, which, slot):
        pltpu.make_async_remote_copy(
            src_ref=buffer.at[0, q], dst_ref=buffer.at[which, slot],
            send_sem=send_sems.at[0], recv_sem=sems.at[which, slot],
            device_id=sibling, device_id_type=MESH,
        ).wait_recv()

    def wait_plane(buffer, sems, slot):
        @pl.when(slot != q)
        def _():
            wait_block(buffer, sems, 0, slot)

    def wait_column(buffer, sems, slot):
        @pl.when(off_diagonal)
        def _():
            wait_block(buffer, sems, 1, slot)

    started = send_block(raw, raw_sems, 0)
    w_copy = pltpu.make_async_remote_copy(
        src_ref=w_proj_ref, dst_ref=w_half, send_sem=w_sems.at[0], recv_sem=w_sems.at[1],
        device_id=sibling, device_id_type=MESH,
    )
    w_copy.start()

    ids = lax.broadcasted_iota(jnp.int32, (length, length), 0)
    lanes = lax.broadcasted_iota(jnp.int32, (length, length), 1)
    flags = jnp.where(ids == lanes, mask_ref[...].astype(jnp.float32), 0.0)
    mask_col[...] = jnp.broadcast_to(jnp.sum(flags, axis=-1, keepdims=True), (length, 2 * half))

    w_copy.wait()
    first_chan = h == 0
    for u in range(2):
        for w in range(4):
            mine = w_proj_ref[u, w].astype(jnp.float32)
            theirs = w_half[u, w].astype(jnp.float32)
            low = jnp.where(first_chan, mine, theirs)
            high = jnp.where(first_chan, theirs, mine)
            full = jnp.concatenate([low, high], axis=-1).astype(jnp.bfloat16)
            w_full[u, w // 2, :, (w % 2) * 2 * half:(w % 2 + 1) * 2 * half] = full

    lower = lax.broadcasted_iota(jnp.int32, (area, 2 * half), 1) < half

    def unpacked(which, pair_slot):
        even = raw[which, chans * pair_slot].astype(jnp.float32)
        odd = raw[which, chans * pair_slot + 1].astype(jnp.float32)
        first = jnp.where(lower, even, pltpu.roll(odd, half, 1))
        second = jnp.where(lower, pltpu.roll(even, half, 1), odd)
        return first, second

    def project(u, side, wide, outer_block, inner_block, keep):
        normed = normalize(
            wide, in_gain_ref[u:u + 1, :], in_bias_ref[u:u + 1, :]
        ).astype(jnp.bfloat16)
        if keep is not None:
            values[keep] = wide.astype(jnp.bfloat16)
            normed_own[keep] = normed
        both = jnp.dot(normed, w_full[u, side], preferred_element_type=jnp.float32)
        outer = mask_col[pl.ds(outer_block * edge, edge), :]
        inner = mask_col[pl.ds(inner_block * edge, edge), :]
        mask = outer[:, None, :] * inner[None, :, :]
        gated = sigmoid(both[:, 2 * half:]) * both[:, :2 * half]
        gated = gated.reshape(edge, edge, 2 * half) * mask
        return gated.astype(jnp.bfloat16).astype(jnp.float32)

    def mix(row_of):
        def step(k, totals):
            tile = tile_op[pl.ds(k * edge, edge), :]
            return tuple(
                totals[i] + spread_op[pl.ds(row_of(i, k), 1), :] * tile for i in range(edge)
            )
        zero = tuple(jnp.zeros((edge, 2 * half), jnp.float32) for _ in range(edge))
        totals = lax.fori_loop(0, length, step, zero, unroll=4)
        return jnp.concatenate(totals, axis=0)

    def finish(u, mixed, block):
        mixed = mixed.astype(jnp.bfloat16).astype(jnp.float32)
        mixed_norm = normalize(
            mixed, out_gain_ref[u:u + 1, :], out_bias_ref[u:u + 1, :]
        ).astype(jnp.bfloat16)
        projected = jnp.dot(mixed_norm, w_out_ref[u], preferred_element_type=jnp.float32)
        gate = sigmoid(jnp.dot(normed_own[block], w_gate_ref[u], preferred_element_type=jnp.float32))
        return (values[block].astype(jnp.float32) + gate * projected).astype(jnp.bfloat16)

    def right_blocks(pair_slot, carry):
        for part in range(chans):
            wait_plane(raw, raw_sems, chans * pair_slot + part)
        for part, wide in enumerate(unpacked(0, pair_slot)):
            inner = chans * pair_slot + part
            gated = project(0, 1, wide, r, inner, None)
            for j in range(edge):
                tile_op[pl.ds(inner * area + j, edge, stride=edge), :] = gated[j]
        return carry

    lax.fori_loop(0, cols, right_blocks, 0)

    def left_blocks(pair_slot, carry):
        for part in range(chans):
            wait_column(raw, raw_sems, chans * pair_slot + part)
        for part, wide in enumerate(unpacked(away, pair_slot)):
            inner = chans * pair_slot + part
            gated = project(0, 0, wide, q, inner, inner)
            for i in range(edge):
                spread_op[pl.ds(i * length + inner * edge, edge), :] = gated[i]
        return carry

    lax.fori_loop(0, cols, left_blocks, 0)
    mid[0, q] = finish(0, mix(lambda i, k: i * length + k), r)

    started += send_block(mid, mid_sems, 2 * blocks)

    def left_columns(slot, carry):
        wait_plane(mid, mid_sems, slot)
        gated = project(1, 0, mid[0, slot].astype(jnp.float32), slot, r, None)
        spread_op[pl.ds(slot * area, area), :] = gated.reshape(area, 2 * half)
        return carry

    lax.fori_loop(0, blocks, left_columns, 0)

    def right_columns(slot, carry):
        wait_column(mid, mid_sems, slot)
        gated = project(1, 1, mid[away, slot].astype(jnp.float32), slot, q, slot)
        tile_op[pl.ds(slot * area, area), :] = gated.reshape(area, 2 * half)
        return carry

    lax.fori_loop(0, blocks, right_columns, 0)
    fin[h] = finish(1, mix(lambda i, k: k * edge + i), r)

    last = pltpu.make_async_remote_copy(
        src_ref=fin.at[h], dst_ref=fin.at[h], send_sem=fin_sems.at[0], recv_sem=fin_sems.at[1],
        device_id=sibling, device_id_type=MESH,
    )
    last.start()
    for copy in started:
        copy.wait_send()
    last.wait()
    for part in range(chans):
        block = fin[part].astype(jnp.float32)
        piece = jnp.where(first_chan, block[:, :half], block[:, half:])
        out_ref[:, part * edge:(part + 1) * edge, :] = (
            piece.reshape(edge, edge, half).astype(jnp.bfloat16)
        )


def local(sizes, pair, token_mask, w_proj, w_gate, w_out, in_gain, in_bias, out_gain, out_bias):
    rows, cols, chans = sizes
    edge, wide_cols, half = pair.shape
    blocks, area, length = rows, edge * edge, token_mask.shape[0]
    full = chans * half
    assert chans == 2 and rows == cols * chans and wide_cols == chans * edge
    vmem = pl.BlockSpec(memory_space=pltpu.VMEM)
    return pl.pallas_call(
        functools.partial(kernel, rows, cols, chans, edge),
        out_shape=jax.ShapeDtypeStruct(pair.shape, pair.dtype),
        in_specs=[vmem] * 9,
        out_specs=vmem,
        scratch_shapes=[
            pltpu.VMEM((2, blocks, area, full), jnp.bfloat16),
            pltpu.VMEM((2, blocks, area, full), jnp.bfloat16),
            pltpu.VMEM((chans, area, full), jnp.bfloat16),
            pltpu.VMEM(w_proj.shape, jnp.bfloat16),
            pltpu.VMEM((2, 2, full, 2 * full), jnp.bfloat16),
            pltpu.VMEM((length, full), jnp.float32),
            pltpu.VMEM((edge * length, full), jnp.float32),
            pltpu.VMEM((edge * length, full), jnp.float32),
            pltpu.VMEM((blocks, area, full), jnp.bfloat16),
            pltpu.VMEM((blocks, area, full), jnp.bfloat16),
            pltpu.SemaphoreType.DMA((4 * blocks,)),
            pltpu.SemaphoreType.DMA((2, blocks)),
            pltpu.SemaphoreType.DMA((2, blocks)),
            pltpu.SemaphoreType.DMA((2,)),
            pltpu.SemaphoreType.DMA((2,)),
        ],
        compiler_params=pltpu.CompilerParams(
            collective_id=0, has_side_effects=True, vmem_limit_bytes=48 * 1024 * 1024
        ),
    )(pair, token_mask.reshape(1, length), w_proj, w_gate, w_out, in_gain, in_bias, out_gain, out_bias)


def solution(mesh):
    sizes = tuple(mesh.shape[name] for name in ("row", "col", "chan"))
    return jax.shard_map(
        functools.partial(local, sizes),
        mesh=mesh,
        in_specs=(
            P(("groups", "row"), "col", "chan"),
            P("groups"),
            P(None, None, None, "chan"),
            P(),
            P(),
            P(),
            P(),
            P(),
            P(),
        ),
        out_specs=P(("groups", "row"), "col", "chan"),
        check_vma=False,
    )
```

time: 149 us -> 26.7 us (0.18)
  blocking collectives: 56.3 us -> 0 us
  waiting for transfers between devices: 53.9 us -> 0 us
  Pallas kernels: 0 us -> 24.6 us
  local copies, waits for them, and re-layouts: 16 us -> 1.82 us
  between operations: 13.4 us -> 0.11 us
  other arithmetic: 4.38 us -> 0 us
  matrix products: 4.27 us -> 0 us
    all_gather x6 -> x0, blocking collectives: 49.8 us -> none  [the longest x1 16.3 us: local(): left_cols = lax.all_gather(left, 'row', axis=0, tiled=True)]
    psum x2 -> x0, waiting for transfers between devices: 39 us -> none  [broadcast(): return lax.psum(kept, axis)]
    pallas_call x0 -> x1, Pallas kernels: none -> 24.6 us  [local(): pl.pallas_call(functools.partial(kernel, rows, cols, chans, edge), out_sh...]
    unnamed x6 -> x0, waiting for transfers between devices: 14.8 us -> none
    unnamed x28 -> x18, local copies, waits for them, and re-layouts: 12 us -> 1.82 us
    psum x2 -> x0, blocking collectives: 6.59 us -> none  [local(): lax.psum((jnp.sum(mixed_wide, axis=-1), jnp.sum(mixed_wide * mixed_wide,...]
    dot_general x8 -> x0, matrix products: 4.27 us -> none  [the longest x2 1.35 us: local(): jnp.einsum('ijc,ce->ije', normed, gate_cols, preferred_element_type=jnp.f...]
    all_gather x4 -> x0, local copies, waits for them, and re-layouts: 2.72 us -> none  [the longest x1 1.59 us: local(): lax.all_gather(right, 'row', axis=0, tiled=True)]
  transfers between devices with their start and end apart: 4 -> 0, of which waited for: 4 -> 0; matrix products, arithmetic and copies ran while one was open for 1% -> 0% of each run, Pallas kernels for 0% -> 0%
where the time goes in v1:
time: 26.7 us; the launch traced here: 26.5 us
  Pallas kernels  24.6 us (92%)
  local copies, waits for them, and re-layouts  1.82 us (7%)
    pallas_call x1, Pallas kernels, local(): pl.pallas_call(functools.partial(kernel, rows, cols, chans, edge), out_sh...  24.6 us
    unnamed x18, local copies, waits for them, and re-layouts  1.82 us

profile of v1, /device:TPU:0, one launch (start us, length us, event | category | flops | bytes accessed | tf_op | source)
XLA Modules:
  0.0 26.5 jit_solution(17616952364725534239)
XLA Ops:
  0.0 0.0 copy-start
  0.0 0.0 copy-start.1
  0.0 0.0 copy-start.2
  0.0 0.0 copy-start.3
  0.0 0.0 copy-start.4
  0.0 0.0 copy-start.5
  0.0 0.0 copy-start.6
  0.0 0.0 copy-start.7
  0.0 1.1 %copy.10.w_proj_ref = bf16[2,4,128,64]{3,2,1,0:T(8,128)(2,1)S(1)} copy(bf16[2,4,128,64]{2,3,1,0:T(8,128)(2,1)} %param.11) | data formatting | bytes 262144 | tf_op args[2]
  1.2 0.0 copy-done
  1.2 0.0 copy-done.1
  1.2 0.0 copy-done.2
  1.2 0.0 copy-done.3
  1.2 0.0 copy-done.4
  1.2 0.0 copy-done.5
  1.2 0.0 copy-done.6
  1.3 0.0 copy-done.7
  1.3 24.6 %shard_map.91 = bf16[16,32,64]{2,1,0:T(8,128)(2,1)S(1)} custom-call(bf16[16,32,64]{2,1,0:T(8,128)(2,1)S(1)} %copy-done, s32[1,64]{1,0:T(1,128)S(1)} %bitcast.1, bf16[2,4,128,64]{3,2,1,0:T(8,128)(2,1)S(1)} %copy.10.w_proj_ref, bf16[2,128,128]{2,1,0:T(8,128)(2,1)S(1)} %copy-done.1, bf16[2,128,128]{2,1,0:T(8,128)(2,1)S(1)} %copy-done.2, ...), custom_call_target="tpu_custom_call" | custom-call | tf_op jit(solution)/shard_map/pallas_call | solution.py:235
  25.9 0.7 %copy.12 = bf16[16,32,64]{2,1,0:T(8,128)(2,1)} copy(bf16[16,32,64]{2,1,0:T(8,128)(2,1)S(1)} %shard_map.91) | data formatting | bytes 131072
Async XLA Ops:
  0.0 1.2 %copy-start = (bf16[16,32,64]{2,1,0:T(8,128)(2,1)S(1)}, bf16[16,32,64]{2,1,0:T(8,128)(2,1)}, u32[]{:S(2)}) copy-start(bf16[16,32,64]{2,1,0:T(8,128)(2,1)} %pair_ref.1) | copy-start | bytes 196612
  0.0 1.2 %copy-start.1 = (bf16[2,128,128]{2,1,0:T(8,128)(2,1)S(1)}, bf16[2,128,128]{2,1,0:T(8,128)(2,1)}, u32[]{:S(2)}) copy-start(bf16[2,128,128]{2,1,0:T(8,128)(2,1)} %w_gate_ref.1) | copy-start | bytes 196612
  0.0 1.2 %copy-start.2 = (bf16[2,128,128]{2,1,0:T(8,128)(2,1)S(1)}, bf16[2,128,128]{2,1,0:T(8,128)(2,1)}, u32[]{:S(2)}) copy-start(bf16[2,128,128]{2,1,0:T(8,128)(2,1)} %w_out_ref.1) | copy-start | bytes 196612
  0.0 1.2 %copy-start.3 = (f32[2,128]{1,0:T(2,128)S(1)}, f32[2,128]{1,0:T(2,128)}, u32[]{:S(2)}) copy-start(f32[2,128]{1,0:T(2,128)} %in_gain_ref.1) | copy-start | bytes 3076
  0.0 1.2 %copy-start.4 = (f32[2,128]{1,0:T(2,128)S(1)}, f32[2,128]{1,0:T(2,128)}, u32[]{:S(2)}) copy-start(f32[2,128]{1,0:T(2,128)} %in_bias_ref.1) | copy-start | bytes 3076
  0.0 1.2 %copy-start.5 = (f32[2,128]{1,0:T(2,128)S(1)}, f32[2,128]{1,0:T(2,128)}, u32[]{:S(2)}) copy-start(f32[2,128]{1,0:T(2,128)} %out_gain_ref.1) | copy-start | bytes 3076
  0.0 1.2 %copy-start.6 = (f32[2,128]{1,0:T(2,128)S(1)}, f32[2,128]{1,0:T(2,128)}, u32[]{:S(2)}) copy-start(f32[2,128]{1,0:T(2,128)} %out_bias_ref.1) | copy-start | bytes 3076
  0.0 1.2 %copy-start.7 = (s32[64]{0:T(128)S(1)}, s32[64]{0:T(128)}, u32[]{:S(2)}) copy-start(s32[64]{0:T(128)} %param.10) | copy-start | bytes 772

commit v2 on v1

--- a/solution.py
+++ b/solution.py
@@ -72,11 +72,12 @@
                 send_sem=send_sems.at[base + step], recv_sem=sems.at[1, q],
                 device_id=column(step), device_id_type=MESH,
             ))
-        for step in range(1, blocks):
+        for step in range(cols):
+            target = (group, r, lax.rem(c + step, cols), h) if step else sibling
             copies.append(pltpu.make_async_remote_copy(
                 src_ref=buffer.at[0, q], dst_ref=buffer.at[0, q],
                 send_sem=send_sems.at[base + blocks + step], recv_sem=sems.at[0, q],
-                device_id=plane(step), device_id_type=MESH,
+                device_id=target, device_id_type=MESH,
             ))
         for copy in copies:
             copy.start()
@@ -89,10 +90,20 @@
             device_id=sibling, device_id_type=MESH,
         ).wait_recv()
 
-    def wait_plane(buffer, sems, slot):
-        @pl.when(slot != q)
-        def _():
+    def hand_on(buffer, sems, base):
+        copies = []
+        for step in range(1, cols):
+            slot = lax.rem(c + step, cols) * chans + h
             wait_block(buffer, sems, 0, slot)
+            copy = pltpu.make_async_remote_copy(
+                src_ref=buffer.at[0, slot], dst_ref=buffer.at[0, slot],
+                send_sem=send_sems.at[base + blocks + cols - 1 + step],
+                recv_sem=sems.at[0, slot],
+                device_id=sibling, device_id_type=MESH,
+            )
+            copy.start()
+            copies.append(copy)
+        return copies
 
     def wait_column(buffer, sems, slot):
         @pl.when(off_diagonal)
@@ -165,9 +176,9 @@
         gate = sigmoid(jnp.dot(normed_own[block], w_gate_ref[u], preferred_element_type=jnp.float32))
         return (values[block].astype(jnp.float32) + gate * projected).astype(jnp.bfloat16)
 
-    def right_blocks(pair_slot, carry):
-        for part in range(chans):
-            wait_plane(raw, raw_sems, chans * pair_slot + part)
+    def right_blocks(step, carry):
+        pair_slot = lax.rem(c + step, cols)
+        wait_block(raw, raw_sems, 0, chans * pair_slot + 1 - h)
         for part, wide in enumerate(unpacked(0, pair_slot)):
             inner = chans * pair_slot + part
             gated = project(0, 1, wide, r, inner, None)
@@ -175,7 +186,9 @@
                 tile_op[pl.ds(inner * area + j, edge, stride=edge), :] = gated[j]
         return carry
 
-    lax.fori_loop(0, cols, right_blocks, 0)
+    right_blocks(0, 0)
+    started += hand_on(raw, raw_sems, 0)
+    lax.fori_loop(1, cols, right_blocks, 0)
 
     def left_blocks(pair_slot, carry):
         for part in range(chans):
@@ -192,13 +205,18 @@
 
     started += send_block(mid, mid_sems, 2 * blocks)
 
-    def left_columns(slot, carry):
-        wait_plane(mid, mid_sems, slot)
-        gated = project(1, 0, mid[0, slot].astype(jnp.float32), slot, r, None)
-        spread_op[pl.ds(slot * area, area), :] = gated.reshape(area, 2 * half)
-        return carry
-
-    lax.fori_loop(0, blocks, left_columns, 0)
+    def left_columns(step, carry):
+        pair_slot = lax.rem(c + step, cols)
+        wait_block(mid, mid_sems, 0, chans * pair_slot + 1 - h)
+        for part in range(chans):
+            slot = chans * pair_slot + part
+            gated = project(1, 0, mid[0, slot].astype(jnp.float32), slot, r, None)
+            spread_op[pl.ds(slot * area, area), :] = gated.reshape(area, 2 * half)
+        return carry
+
+    left_columns(0, 0)
+    started += hand_on(mid, mid_sems, 2 * blocks)
+    lax.fori_loop(1, cols, left_columns, 0)
 
     def right_columns(slot, carry):
         wait_column(mid, mid_sems, slot)

time: 26.7 us -> 25.6 us (0.959)
  Pallas kernels: 24.6 us -> 23.5 us
    pallas_call x1, Pallas kernels: 24.6 us -> 23.5 us  [local(): pl.pallas_call(functools.partial(kernel, rows, cols, chans, edge), out_sh...]
where the time goes in v2:
time: 25.6 us; the launch traced here: 25.5 us
  Pallas kernels  23.5 us (92%)
  local copies, waits for them, and re-layouts  1.82 us (7%)
    pallas_call x1, Pallas kernels, local(): pl.pallas_call(functools.partial(kernel, rows, cols, chans, edge), out_sh...  23.5 us
    unnamed x18, local copies, waits for them, and re-layouts  1.82 us

profile of v2, /device:TPU:0, one launch (start us, length us, event | category | flops | bytes accessed | tf_op | source)
XLA Modules:
  0.0 25.5 jit_solution(9885613696202143077)
XLA Ops:
  0.0 0.0 copy-start
  0.0 0.0 copy-start.1
  0.0 0.0 copy-start.2
  0.0 0.0 copy-start.3
  0.0 0.0 copy-start.4
  0.0 0.0 copy-start.5
  0.0 0.0 copy-start.6
  0.0 0.0 copy-start.7
  0.0 1.1 %copy.10.w_proj_ref = bf16[2,4,128,64]{3,2,1,0:T(8,128)(2,1)S(1)} copy(bf16[2,4,128,64]{2,3,1,0:T(8,128)(2,1)} %param.11) | data formatting | bytes 262144 | tf_op args[2]
  1.2 0.0 copy-done
  1.2 0.0 copy-done.1
  1.2 0.0 copy-done.2
  1.2 0.0 copy-done.3
  1.2 0.0 copy-done.4
  1.2 0.0 copy-done.5
  1.2 0.0 copy-done.6
  1.3 0.0 copy-done.7
  1.3 23.5 %shard_map.91 = bf16[16,32,64]{2,1,0:T(8,128)(2,1)S(1)} custom-call(bf16[16,32,64]{2,1,0:T(8,128)(2,1)S(1)} %copy-done, s32[1,64]{1,0:T(1,128)S(1)} %bitcast.1, bf16[2,4,128,64]{3,2,1,0:T(8,128)(2,1)S(1)} %copy.10.w_proj_ref, bf16[2,128,128]{2,1,0:T(8,128)(2,1)S(1)} %copy-done.1, bf16[2,128,128]{2,1,0:T(8,128)(2,1)S(1)} %copy-done.2, ...), custom_call_target="tpu_custom_call" | custom-call | tf_op jit(solution)/shard_map/pallas_call | solution.py:253
  24.8 0.7 %copy.12 = bf16[16,32,64]{2,1,0:T(8,128)(2,1)} copy(bf16[16,32,64]{2,1,0:T(8,128)(2,1)S(1)} %shard_map.91) | data formatting | bytes 131072
Async XLA Ops:
  0.0 1.2 %copy-start = (bf16[16,32,64]{2,1,0:T(8,128)(2,1)S(1)}, bf16[16,32,64]{2,1,0:T(8,128)(2,1)}, u32[]{:S(2)}) copy-start(bf16[16,32,64]{2,1,0:T(8,128)(2,1)} %pair_ref.1) | copy-start | bytes 196612
  0.0 1.2 %copy-start.1 = (bf16[2,128,128]{2,1,0:T(8,128)(2,1)S(1)}, bf16[2,128,128]{2,1,0:T(8,128)(2,1)}, u32[]{:S(2)}) copy-start(bf16[2,128,128]{2,1,0:T(8,128)(2,1)} %w_gate_ref.1) | copy-start | bytes 196612
  0.0 1.2 %copy-start.2 = (bf16[2,128,128]{2,1,0:T(8,128)(2,1)S(1)}, bf16[2,128,128]{2,1,0:T(8,128)(2,1)}, u32[]{:S(2)}) copy-start(bf16[2,128,128]{2,1,0:T(8,128)(2,1)} %w_out_ref.1) | copy-start | bytes 196612
  0.0 1.2 %copy-start.3 = (f32[2,128]{1,0:T(2,128)S(1)}, f32[2,128]{1,0:T(2,128)}, u32[]{:S(2)}) copy-start(f32[2,128]{1,0:T(2,128)} %in_gain_ref.1) | copy-start | bytes 3076
  0.0 1.2 %copy-start.4 = (f32[2,128]{1,0:T(2,128)S(1)}, f32[2,128]{1,0:T(2,128)}, u32[]{:S(2)}) copy-start(f32[2,128]{1,0:T(2,128)} %in_bias_ref.1) | copy-start | bytes 3076
  0.0 1.2 %copy-start.5 = (f32[2,128]{1,0:T(2,128)S(1)}, f32[2,128]{1,0:T(2,128)}, u32[]{:S(2)}) copy-start(f32[2,128]{1,0:T(2,128)} %out_gain_ref.1) | copy-start | bytes 3076
  0.0 1.2 %copy-start.6 = (f32[2,128]{1,0:T(2,128)S(1)}, f32[2,128]{1,0:T(2,128)}, u32[]{:S(2)}) copy-start(f32[2,128]{1,0:T(2,128)} %out_bias_ref.1) | copy-start | bytes 3076
  0.0 1.2 %copy-start.7 = (s32[64]{0:T(128)S(1)}, s32[64]{0:T(128)}, u32[]{:S(2)}) copy-start(s32[64]{0:T(128)} %param.10) | copy-start | bytes 772

commit v3 on v2

--- a/solution.py
+++ b/solution.py
@@ -66,18 +66,18 @@
 
     def send_block(buffer, sems, base):
         copies = []
-        for step in range(1, blocks):
-            copies.append(pltpu.make_async_remote_copy(
-                src_ref=buffer.at[0, q], dst_ref=buffer.at[1, q],
-                send_sem=send_sems.at[base + step], recv_sem=sems.at[1, q],
-                device_id=column(step), device_id_type=MESH,
-            ))
         for step in range(cols):
             target = (group, r, lax.rem(c + step, cols), h) if step else sibling
             copies.append(pltpu.make_async_remote_copy(
                 src_ref=buffer.at[0, q], dst_ref=buffer.at[0, q],
                 send_sem=send_sems.at[base + blocks + step], recv_sem=sems.at[0, q],
                 device_id=target, device_id_type=MESH,
+            ))
+        for step in range(1, blocks):
+            copies.append(pltpu.make_async_remote_copy(
+                src_ref=buffer.at[0, q], dst_ref=buffer.at[1, q],
+                send_sem=send_sems.at[base + step], recv_sem=sems.at[1, q],
+                device_id=column(step), device_id_type=MESH,
             ))
         for copy in copies:
             copy.start()
@@ -164,7 +164,7 @@
                 totals[i] + spread_op[pl.ds(row_of(i, k), 1), :] * tile for i in range(edge)
             )
         zero = tuple(jnp.zeros((edge, 2 * half), jnp.float32) for _ in range(edge))
-        totals = lax.fori_loop(0, length, step, zero, unroll=4)
+        totals = lax.fori_loop(0, length, step, zero, unroll=8)
         return jnp.concatenate(totals, axis=0)
 
     def finish(u, mixed, block):

time: 25.6 us -> 25.4 us (level)
  no operation moved by 1% of the time
where the time goes in v3:
time: 25.4 us; the launch traced here: 25.3 us
  Pallas kernels  23.3 us (92%)
  local copies, waits for them, and re-layouts  1.82 us (7%)
    pallas_call x1, Pallas kernels, local(): pl.pallas_call(functools.partial(kernel, rows, cols, chans, edge), out_sh...  23.3 us
    unnamed x18, local copies, waits for them, and re-layouts  1.82 us

profile of v3, /device:TPU:0, one launch (start us, length us, event | category | flops | bytes accessed | tf_op | source)
XLA Modules:
  0.0 25.3 jit_solution(12588929113252639197)
XLA Ops:
  0.0 0.0 copy-start
  0.0 0.0 copy-start.1
  0.0 0.0 copy-start.2
  0.0 0.0 copy-start.3
  0.0 0.0 copy-start.4
  0.0 0.0 copy-start.5
  0.0 0.0 copy-start.6
  0.0 0.0 copy-start.7
  0.0 1.1 %copy.10.w_proj_ref = bf16[2,4,128,64]{3,2,1,0:T(8,128)(2,1)S(1)} copy(bf16[2,4,128,64]{2,3,1,0:T(8,128)(2,1)} %param.11) | data formatting | bytes 262144 | tf_op args[2]
  1.2 0.0 copy-done
  1.2 0.0 copy-done.1
  1.2 0.0 copy-done.2
  1.2 0.0 copy-done.3
  1.2 0.0 copy-done.4
  1.2 0.0 copy-done.5
  1.2 0.0 copy-done.6
  1.3 0.0 copy-done.7
  1.3 23.3 %shard_map.91 = bf16[16,32,64]{2,1,0:T(8,128)(2,1)S(1)} custom-call(bf16[16,32,64]{2,1,0:T(8,128)(2,1)S(1)} %copy-done, s32[1,64]{1,0:T(1,128)S(1)} %bitcast.1, bf16[2,4,128,64]{3,2,1,0:T(8,128)(2,1)S(1)} %copy.10.w_proj_ref, bf16[2,128,128]{2,1,0:T(8,128)(2,1)S(1)} %copy-done.1, bf16[2,128,128]{2,1,0:T(8,128)(2,1)S(1)} %copy-done.2, ...), custom_call_target="tpu_custom_call" | custom-call | tf_op jit(solution)/shard_map/pallas_call | solution.py:253
  24.6 0.7 %copy.12 = bf16[16,32,64]{2,1,0:T(8,128)(2,1)} copy(bf16[16,32,64]{2,1,0:T(8,128)(2,1)S(1)} %shard_map.91) | data formatting | bytes 131072
Async XLA Ops:
  0.0 1.2 %copy-start = (bf16[16,32,64]{2,1,0:T(8,128)(2,1)S(1)}, bf16[16,32,64]{2,1,0:T(8,128)(2,1)}, u32[]{:S(2)}) copy-start(bf16[16,32,64]{2,1,0:T(8,128)(2,1)} %pair_ref.1) | copy-start | bytes 196612
  0.0 1.2 %copy-start.1 = (bf16[2,128,128]{2,1,0:T(8,128)(2,1)S(1)}, bf16[2,128,128]{2,1,0:T(8,128)(2,1)}, u32[]{:S(2)}) copy-start(bf16[2,128,128]{2,1,0:T(8,128)(2,1)} %w_gate_ref.1) | copy-start | bytes 196612
  0.0 1.2 %copy-start.2 = (bf16[2,128,128]{2,1,0:T(8,128)(2,1)S(1)}, bf16[2,128,128]{2,1,0:T(8,128)(2,1)}, u32[]{:S(2)}) copy-start(bf16[2,128,128]{2,1,0:T(8,128)(2,1)} %w_out_ref.1) | copy-start | bytes 196612
  0.0 1.2 %copy-start.3 = (f32[2,128]{1,0:T(2,128)S(1)}, f32[2,128]{1,0:T(2,128)}, u32[]{:S(2)}) copy-start(f32[2,128]{1,0:T(2,128)} %in_gain_ref.1) | copy-start | bytes 3076
  0.0 1.2 %copy-start.4 = (f32[2,128]{1,0:T(2,128)S(1)}, f32[2,128]{1,0:T(2,128)}, u32[]{:S(2)}) copy-start(f32[2,128]{1,0:T(2,128)} %in_bias_ref.1) | copy-start | bytes 3076
  0.0 1.2 %copy-start.5 = (f32[2,128]{1,0:T(2,128)S(1)}, f32[2,128]{1,0:T(2,128)}, u32[]{:S(2)}) copy-start(f32[2,128]{1,0:T(2,128)} %out_gain_ref.1) | copy-start | bytes 3076
  0.0 1.2 %copy-start.6 = (f32[2,128]{1,0:T(2,128)S(1)}, f32[2,128]{1,0:T(2,128)}, u32[]{:S(2)}) copy-start(f32[2,128]{1,0:T(2,128)} %out_bias_ref.1) | copy-start | bytes 3076
  0.0 1.2 %copy-start.7 = (s32[64]{0:T(128)S(1)}, s32[64]{0:T(128)}, u32[]{:S(2)}) copy-start(s32[64]{0:T(128)} %param.10) | copy-start | bytes 772
